TPU v7x, 32 devices: a whole 2x2x4 slice. The times are simulated.
32 devices in a mesh: win: 2 (over x), chan: 16 (over z, y, core).
Axes of the slice: x: 2, y: 2, z: 4, core: 2. Of those that a mesh axis runs over, the one named last changes fastest.
Arguments:
- spectra: bfloat16 [8, 256, 2, 2048], P('win', 'chan')
- window_gain: float32 [8], P('win'), may hold values from 0.4 to 3
- dead_mask: int32 [8, 256], P('win', 'chan'), may hold values 0 or 1
- order: int32 [256], replicated, may hold values from 0 to 15
Outputs:
- stack: bfloat16 [256, 256, 2, 2048], P(None, 'chan', None, 'win')
- window_weight: float32 [8], P('win')
All inputs are finite; a program needn't handle non-finite values. No bound on the sum of `dead_mask` on one device may be relied on, other than what follows from the above.
Results may differ from a plain program's by a relative error of at most 0.0064.
Values may be sent and summed in bfloat16 or wider, within the bound.
A program may use at most 128 MiB of HBM per device.

v0:
```python
import jax
import jax.numpy as jnp
from jax import lax
from jax.sharding import PartitionSpec as P

ITERS = 2


def solve_stack(src_re, src_im, ch_re, ch_im, cells):
    f32 = jnp.float32
    bf16 = jnp.bfloat16
    corr_form = "ksf,kcf->scf"
    proj_form = "ksf,scf->kcf"
    row_axis = 1
    freq_axis = 1
    cross_axes = (1, 2)
    count = src_re.shape[0]
    a_square = jnp.sum(
        jnp.square(src_re.astype(f32)) + jnp.square(src_im.astype(f32)), axis=row_axis
    )
    b_square = jnp.sum(jnp.square(ch_re.astype(f32)) + jnp.square(ch_im.astype(f32)), axis=row_axis)
    energy = jnp.sum(a_square * b_square, axis=freq_axis)

    def product(form, left, right):
        return jnp.einsum(form, left, right, preferred_element_type=f32)

    def stack_of(weight):
        shaped = weight[:, None, None]
        w_re = (shaped * ch_re.astype(f32)).astype(bf16)
        w_im = (shaped * ch_im.astype(f32)).astype(bf16)
        total = jnp.sum(weight)
        gre = (product(corr_form, src_re, w_re) + product(corr_form, src_im, w_im)) / total
        gim = (product(corr_form, src_re, w_im) - product(corr_form, src_im, w_re)) / total
        return (gre.astype(bf16), gim.astype(bf16))

    weight = jnp.ones((count,), f32)
    for step in range(ITERS):
        gre, gim = stack_of(weight)
        p_re = product(proj_form, src_re, gre) - product(proj_form, src_im, gim)
        p_im = product(proj_form, src_re, gim) + product(proj_form, src_im, gre)
        cross = jnp.sum(ch_re.astype(f32) * p_re + ch_im.astype(f32) * p_im, axis=cross_axes)
        power = jnp.sum(jnp.square(gre.astype(f32)) + jnp.square(gim.astype(f32)))
        partial_misfit = energy - 2.0 * cross + power
        misfit = lax.psum(partial_misfit, ("win", "chan"))
        weight = 1.0 / jnp.sqrt(misfit / cells + 1e-06)
    gre, gim = stack_of(weight)
    return (gre, gim, weight)


def body(spectra, window_gain, dead_mask, order):
    f32 = jnp.float32
    bf16 = jnp.bfloat16
    scaled = (
        dead_mask.astype(f32)[:, :, None, None]
        * window_gain[:, None, None, None]
        * spectra.astype(f32)
    ).astype(bf16)
    sources = order.shape[0]
    per_dev = sources // lax.axis_size("chan")
    channels = spectra.shape[1]
    cells = sources * channels * lax.axis_size("chan") * spectra.shape[3]
    local = lax.all_to_all(scaled, "win", split_axis=3, concat_axis=0, tiled=True)
    first = lax.axis_index("chan") * per_dev
    mine = lax.dynamic_slice_in_dim(order, first, per_dev, 0)
    picked = jnp.take(local, mine, axis=1)
    gathered = lax.all_gather(picked, "chan", axis=1, tiled=True)
    gre, gim, weight = solve_stack(
        gathered[:, :, 0, :], gathered[:, :, 1, :], local[:, :, 0, :], local[:, :, 1, :], cells
    )
    stack = jnp.stack([gre, gim], axis=2)
    count = weight.shape[0]
    normed = weight * (count / jnp.sum(weight))
    first_window = lax.axis_index("win") * spectra.shape[0]
    window_weight = lax.dynamic_slice_in_dim(normed, first_window, spectra.shape[0], 0)
    return (stack, window_weight)


def solution(mesh):
    placed = (P("win", "chan", None, None), P("win"), P("win", "chan"), P())
    return jax.shard_map(
        body,
        mesh=mesh,
        in_specs=placed,
        out_specs=(P(None, "chan", None, "win"), P("win")),
        check_vma=False,
    )
```

profile of v0, /device:TPU:0, one launch (start us, length us, event | category | flops | bytes accessed | tf_op | source)
XLA Modules:
  0.0 486.9 jit_solution(12815705863949244203)
XLA Ops:
  7.2 0.8 convert_multiply_fusion.10
  7.9 1.5 multiply_convert_fusion.2
  9.4 4.8 copy.22
  14.2 6.6 %reshape.25 = bf16[2,2,65536]{2,1,0:T(2,128)(2,1)} reshape(bf16[2048,2,4,16]{3,2,1,0:T(4,128)(2,1)} %bitcast.168) | data formatting | bytes 1048576
  20.8 4.2 all-to-all-start
  25.0 0.3 all-gather.2.cloned.1.call-start
  25.4 8.3 %all-to-all-done = bf16[2,2,65536]{2,1,0:T(2,128)(2,1)S(1)} async-done(((bf16[2,2,65536]{2,1,0:T(2,128)(2,1)}), bf16[2,2,65536]{2,1,0:T(2,128)(2,1)S(1)}, u32[]{:S(2)}, u32[]{:S(2)}) %all-to-all-start) | async-done | bytes 524320 | tf_op jit(solution)/shard_map/all_to_all | solution.py:62
  33.8 4.1 reshape.26
  37.9 5.6 %copy.23 = bf16[4,16,2,2,1024]{1,0,3,4,2:T(4,128)(2,1)} copy(bf16[4,16,2,2,1024]{1,0,2,4,3:T(4,128)(2,1)} %bitcast.169) | data formatting | bytes 1048576 | tf_op jit(solution)/shard_map/all_to_all | solution.py:62
  43.5 4.9 %copy.24 = bf16[8,16,2,1024]{3,0,2,1:T(8,128)(2,1)S(1)} copy(bf16[8,16,2,1024]{1,0,3,2:T(8,128)(2,1)} %bitcast.152) | data formatting | bytes 1048576 | tf_op jit(solution)/shard_map/all_to_all | solution.py:62
  48.4 0.6 gather_fusion
  49.0 0.9 select_bitcast_fusion
  49.9 3.4 fusion.19
  53.3 72.2 %all-gather.2.cloned.1.call-done = bf16[8,256,2,1024]{3,0,2,1:T(8,128)(2,1)} async-done(((bf16[8,16,2,1024]{3,0,2,1:T(8,128)(2,1)}), bf16[8,256,2,1024]{3,0,2,1:T(8,128)(2,1)}) %all-gather.2.cloned.1.call-update) | async-done | bytes 8388624 | tf_op jit(solution)/shard_map/all_gather | solution.py:66
  125.6 6.0 %fusion.72 = (bf16[8,256,1,1024]{3,0,2,1:T(8,128)(2,1)}, bf16[8,256,1,1024]{3,0,2,1:T(8,128)(2,1)}) fusion(bf16[8,256,2,1024]{3,0,2,1:T(8,128)(2,1)} %all-gather.2.cloned.1.call-done), kind=kLoop, calls=%fused_computation.91 | loop fusion | bytes 16777216 | tf_op jit(solution)/shard_map/slice | solution.py:68
  131.6 7.3 %copy.28 = bf16[8,256,1,1024]{1,0,3,2:T(8,128)(2,1)} copy(bf16[8,256,1,1024]{3,0,2,1:T(8,128)(2,1)} %get-tuple-element.12) | data formatting | bytes 8388608
  138.8 10.1 %fusion.52 = f32[1024,16,256]{2,1,0:T(8,128)} fusion(bf16[8,256,1,1024]{1,0,3,2:T(8,128)(2,1)} %copy.28, bf16[8,16,2,1024]{1,0,3,2:T(8,128)(2,1)} %bitcast.154), kind=kOutput, calls=%fused_computation.73 | convolution fusion | flops 67108864 | bytes 23068672 | tf_op jit(solution)/shard_map/ksf,kcf->scf/dot_general | solution.py:25
  148.9 6.7 %fusion.49 = f32[1024,16,256]{2,1,0:T(8,128)} fusion(bf16[8,256,1,1024]{1,0,3,2:T(8,128)(2,1)S(1)} %copy-done, bf16[8,16,2,1024]{1,0,3,2:T(8,128)(2,1)S(1)} %bitcast.163), kind=kOutput, calls=%fused_computation.70 | convolution fusion | flops 67108864 | bytes 23068672 | tf_op jit(solution)/shard_map/ksf,kcf->scf/dot_general | solution.py:25
  155.6 7.3 %copy.29 = bf16[8,256,1,1024]{1,0,3,2:T(8,128)(2,1)} copy(bf16[8,256,1,1024]{3,0,2,1:T(8,128)(2,1)} %get-tuple-element.13) | data formatting | bytes 8388608
  163.0 5.3 %add_reduce_fusion.2 = f32[8,1024]{0,1:T(8,128)S(1)} fusion(bf16[8,256,1,1024]{1,0,3,2:T(8,128)(2,1)} %copy.29, bf16[8,256,1,1024]{1,0,3,2:T(8,128)(2,1)} %copy.28), kind=kLoop, calls=%fused_computation.36 | loop fusion | flops 12574720 | bytes 8421376 | tf_op jit(solution)/shard_map/reduce_sum | solution.py:18
  168.3 10.9 %multiply_convert_fusion.1 = bf16[1024,16,256]{2,1,0:T(8,128)(2,1)} fusion(f32[1024,16,256]{2,1,0:T(8,128)} %fusion.52, bf16[8,256,1,1024]{1,0,3,2:T(8,128)(2,1)S(1)} %copy-done.5, bf16[8,16,2,1024]{1,0,3,2:T(8,128)(2,1)} %bitcast.155), kind=kOutput, calls=%fused_computation.9 | convolution fusion | flops 79691776 | bytes 31457280 | tf_op jit(solution)/shard_map/ksf,kcf->scf/dot_general | solution.py:25
  179.2 7.7 %fusion.12 = f32[1024,16,8]{1,2,0:T(8,128)} fusion(bf16[1024,16,256]{2,1,0:T(8,128)(2,1)} %multiply_convert_fusion.1, bf16[8,256,1,1024]{1,0,3,2:T(8,128)(2,1)S(1)} %copy-done.5), kind=kOutput, calls=%fused_computation.22 | convolution fusion | flops 67108864 | bytes 13107200 | tf_op jit(solution)/shard_map/ksf,scf->kcf/dot_general | solution.py:25
  186.8 16.6 %add_reduce_fusion.1 = (f32[]{:T(128)}, bf16[1024,16,256]{2,1,0:T(8,128)(2,1)}) fusion(bf16[1024,16,256]{2,1,0:T(8,128)(2,1)} %multiply_convert_fusion.1, f32[1024,16,256]{2,1,0:T(8,128)} %fusion.49, bf16[8,256,1,1024]{1,0,3,2:T(8,128)(2,1)} %copy.29, bf16[8,16,2,1024]{1,0,3,2:T(8,128)(2,1)} %bitcast.156), kind=kOutput, calls=%fused_computation.7 | convolution fusion | flops 104857600 | bytes 39845892 | tf_op jit(solution)/shard_map/ksf,kcf->scf/dot_general | solution.py:25
  203.4 8.8 %fusion.8 = f32[1024,16,8]{1,2,0:T(8,128)} fusion(bf16[1024,16,256]{2,1,0:T(8,128)(2,1)} %get-tuple-element.19, bf16[8,256,1,1024]{1,0,3,2:T(8,128)(2,1)} %copy.28), kind=kOutput, calls=%fused_computation.18 | convolution fusion | flops 67108864 | bytes 13107200 | tf_op jit(solution)/shard_map/ksf,scf->kcf/dot_general | solution.py:25
  212.2 9.0 %fusion.10 = f32[1024,16,8]{1,2,0:T(8,128)} fusion(bf16[1024,16,256]{2,1,0:T(8,128)(2,1)} %get-tuple-element.19, bf16[8,256,1,1024]{1,0,3,2:T(8,128)(2,1)} %copy.29), kind=kOutput, calls=%fused_computation.20 | convolution fusion | flops 67108864 | bytes 13107200 | tf_op jit(solution)/shard_map/ksf,scf->kcf/dot_general | solution.py:25
  221.2 0.2 multiply_reduce_fusion
  221.3 9.7 %fusion.21 = f32[8]{0:T(128)S(1)} fusion(f32[1024,16,8]{1,2,0:T(8,128)} %fusion.8, f32[1024,16,8]{1,2,0:T(8,128)} %fusion.12, f32[1024,16,8]{1,2,0:T(8,128)} %fusion.10, bf16[8,256,1,1024]{1,0,3,2:T(8,128)(2,1)S(1)} %copy-done.1, bf16[1024,16,256]{2,1,0:T(8,128)(2,1)} %multiply_convert_fusion.1, bf16[8,16,2,1024]{1,0,3,2:T(8,128)(2,1)} %bitcast.157), kind=kOutput, calls=%fused_computation.42 | convolution fusion | flops 68157432 | bytes 14680096 | tf_op jit(solution)/shard_map/ksf,scf->kcf/dot_general | solution.py:25
  231.0 0.7 subtract_add_fusion.1
  231.6 38.8 %psum.14 = f32[8]{0:T(128)S(1)} all-reduce(f32[8]{0:T(128)S(1)} %subtract_add_fusion.1), channel_id=1, replica_groups=mesh['win'=2,'chan'=16] {'win','chan'}, use_global_device_ids=true, to_apply=%region_5.6 | all-reduce | flops 8 | bytes 64 | tf_op jit(solution)/shard_map/psum | solution.py:44
  270.4 0.6 fusion.70
  271.0 10.2 %fusion.46 = f32[1024,16,256]{2,1,0:T(8,128)} fusion(bf16[8,256,1,1024]{1,0,3,2:T(8,128)(2,1)} %copy.28, f32[8]{0:T(128)S(1)} %get-tuple-element.17, bf16[8,16,2,1024]{1,0,3,2:T(8,128)(2,1)} %bitcast.158), kind=kOutput, calls=%fused_computation.67 | convolution fusion | flops 67502080 | bytes 23068704 | tf_op jit(solution)/shard_map/ksf,kcf->scf/dot_general | solution.py:25
  281.2 6.9 %fusion.43 = f32[1024,16,256]{2,1,0:T(8,128)} fusion(bf16[8,256,1,1024]{1,0,3,2:T(8,128)(2,1)S(1)} %copy-done.2, f32[8]{0:T(128)S(1)} %get-tuple-element.17, bf16[8,16,2,1024]{1,0,3,2:T(8,128)(2,1)S(1)} %bitcast.164), kind=kOutput, calls=%fused_computation.64 | convolution fusion | flops 67502080 | bytes 23069184 | tf_op jit(solution)/shard_map/ksf,kcf->scf/dot_general | solution.py:25
  288.1 10.7 %divide_convert_fusion.3 = bf16[1024,16,256]{2,1,0:T(8,128)(2,1)} fusion(f32[1024,16,256]{2,1,0:T(8,128)} %fusion.46, f32[]{:T(128)} %get-tuple-element.16, bf16[8,256,1,1024]{1,0,3,2:T(8,128)(2,1)S(1)} %copy-done.6, f32[8]{0:T(128)S(1)} %get-tuple-element.17, bf16[8,16,2,1024]{1,0,3,2:T(8,128)(2,1)} %bitcast.159), kind=kOutput, calls=%fused_computation.6 | convolution fusion | flops 80084992 | bytes 31457824 | tf_op jit(solution)/shard_map/ksf,kcf->scf/dot_general | solution.py:25
  298.8 7.7 %fusion.4 = f32[1024,16,8]{1,2,0:T(8,128)} fusion(bf16[1024,16,256]{2,1,0:T(8,128)(2,1)} %divide_convert_fusion.3, bf16[8,256,1,1024]{1,0,3,2:T(8,128)(2,1)S(1)} %copy-done.6), kind=kOutput, calls=%fused_computation.14 | convolution fusion | flops 67108864 | bytes 13107200 | tf_op jit(solution)/shard_map/ksf,scf->kcf/dot_general | solution.py:25
  306.5 17.5 %add_reduce_fusion = (f32[]{:T(128)}, bf16[1024,16,256]{2,1,0:T(8,128)(2,1)}) fusion(bf16[1024,16,256]{2,1,0:T(8,128)(2,1)} %divide_convert_fusion.3, f32[]{:T(128)} %get-tuple-element.16, f32[1024,16,256]{2,1,0:T(8,128)} %fusion.43, bf16[8,256,1,1024]{1,0,3,2:T(8,128)(2,1)} %copy.29, f32[8]{0:T(128)S(1)} %get-tuple-element.17, ...), kind=kOutput, calls=%fused_computation.4 | convolution fusion | flops 105250816 | bytes 39846436 | tf_op jit(solution)/shard_map/ksf,kcf->scf/dot_general | solution.py:25
  324.0 8.8 %fusion = f32[1024,16,8]{1,2,0:T(8,128)} fusion(bf16[1024,16,256]{2,1,0:T(8,128)(2,1)} %get-tuple-element.21, bf16[8,256,1,1024]{1,0,3,2:T(8,128)(2,1)} %copy.28), kind=kOutput, calls=%fused_computation.10 | convolution fusion | flops 67108864 | bytes 13107200 | tf_op jit(solution)/shard_map/ksf,scf->kcf/dot_general | solution.py:25
  332.8 9.0 %fusion.2 = f32[1024,16,8]{1,2,0:T(8,128)} fusion(bf16[1024,16,256]{2,1,0:T(8,128)(2,1)} %get-tuple-element.21, bf16[8,256,1,1024]{1,0,3,2:T(8,128)(2,1)} %copy.29), kind=kOutput, calls=%fused_computation.12 | convolution fusion | flops 67108864 | bytes 13107200 | tf_op jit(solution)/shard_map/ksf,scf->kcf/dot_general | solution.py:25
  341.7 9.7 %fusion.24 = f32[8]{0:T(128)S(1)} fusion(f32[1024,16,8]{1,2,0:T(8,128)} %fusion, f32[1024,16,8]{1,2,0:T(8,128)} %fusion.4, f32[1024,16,8]{1,2,0:T(8,128)} %fusion.2, bf16[8,256,1,1024]{1,0,3,2:T(8,128)(2,1)S(1)} %copy-done.3, bf16[1024,16,256]{2,1,0:T(8,128)(2,1)} %divide_convert_fusion.3, bf16[8,16,2,1024]{1,0,3,2:T(8,128)(2,1)} %bitcast.161), kind=kOutput, calls=%fused_computation.45 | convolution fusion | flops 68157432 | bytes 14680096 | tf_op jit(solution)/shard_map/ksf,scf->kcf/dot_general | solution.py:25
  351.4 0.6 subtract_add_fusion
  352.0 40.6 %psum.15 = f32[8]{0:T(128)S(1)} all-reduce(f32[8]{0:T(128)S(1)} %subtract_add_fusion), channel_id=1, replica_groups=mesh['win'=2,'chan'=16] {'win','chan'}, use_global_device_ids=true, to_apply=%region_9.10 | all-reduce | flops 8 | bytes 64 | tf_op jit(solution)/shard_map/psum | solution.py:44
  392.6 0.6 fusion.71
  393.9 10.0 %fusion.38 = f32[1024,16,256]{2,1,0:T(8,128)} fusion(bf16[8,256,1,1024]{1,0,3,2:T(8,128)(2,1)} %copy.28, f32[8]{0:T(128)S(1)} %get-tuple-element.15, bf16[8,16,2,1024]{1,0,3,2:T(8,128)(2,1)} %bitcast.162), kind=kOutput, calls=%fused_computation.59 | convolution fusion | flops 67502080 | bytes 23068704 | tf_op jit(solution)/shard_map/ksf,kcf->scf/dot_general | solution.py:25
  403.9 6.9 %fusion.40 = f32[1024,16,256]{2,1,0:T(8,128)} fusion(bf16[8,256,1,1024]{1,0,3,2:T(8,128)(2,1)S(1)} %copy-done.4, f32[8]{0:T(128)S(1)} %get-tuple-element.15, bf16[8,16,2,1024]{1,0,3,2:T(8,128)(2,1)S(1)} %bitcast.165), kind=kOutput, calls=%fused_computation.61 | convolution fusion | flops 67502080 | bytes 23069184 | tf_op jit(solution)/shard_map/ksf,kcf->scf/dot_general | solution.py:25
  410.8 11.8 %fusion.17 = bf16[256,16,1,1024]{0,1,3,2:T(8,128)(2,1)} fusion(f32[]{:T(128)} %fusion.71, f32[1024,16,256]{2,1,0:T(8,128)} %fusion.38, bf16[8,256,1,1024]{1,0,3,2:T(8,128)(2,1)S(1)} %copy-done.7, f32[8]{0:T(128)S(1)} %get-tuple-element.15, bf16[8,16,2,1024]{1,0,3,2:T(8,128)(2,1)S(1)} %bitcast.166), kind=kOutput, calls=%fused_computation.38 | convolution fusion | flops 80084992 | bytes 31457796 | tf_op jit(solution)/shard_map/ksf,kcf->scf/dot_general | solution.py:25
  422.6 11.8 %fusion.16 = bf16[256,16,1,1024]{0,1,3,2:T(8,128)(2,1)} fusion(f32[]{:T(128)} %fusion.71, f32[1024,16,256]{2,1,0:T(8,128)} %fusion.40, bf16[8,256,1,1024]{1,0,3,2:T(8,128)(2,1)S(1)} %copy-done.7, f32[8]{0:T(128)S(1)} %get-tuple-element.15, bf16[8,16,2,1024]{1,0,3,2:T(8,128)(2,1)S(1)} %bitcast.167), kind=kOutput, calls=%fused_computation.37 | convolution fusion | flops 80084992 | bytes 31457796 | tf_op jit(solution)/shard_map/ksf,kcf->scf/dot_general | solution.py:25
  434.5 13.7 %pad_maximum_fusion = bf16[256,16,2,1024]{0,1,3,2:T(8,128)(2,1)} fusion(bf16[256,16,1,1024]{0,1,3,2:T(8,128)(2,1)} %fusion.17, bf16[256,16,1,1024]{0,1,3,2:T(8,128)(2,1)} %fusion.16), kind=kLoop, calls=%fused_computation.1 | loop fusion | flops 8388608 | bytes 33554432 | tf_op jit(solution)/shard_map/stack | solution.py:70
  448.2 31.0 %copy.27 = bf16[256,16,2,1024]{3,2,1,0:T(2,128)(2,1)} copy(bf16[256,16,2,1024]{0,1,3,2:T(8,128)(2,1)} %pad_maximum_fusion) | data formatting | bytes 33554432
  479.2 0.6 dynamic_slice.7
  (28 shorter events, 0.2 us)
Async XLA Ops:
  9.4 15.9 %copy-start.11 = (s32[256]{0:T(256)S(1)}, s32[256]{0:T(256)}, u32[]{:S(2)}) copy-start(s32[256]{0:T(256)} %param.7) | copy-start | bytes 3076
  20.8 12.9 %all-to-all-start = ((bf16[2,2,65536]{2,1,0:T(2,128)(2,1)}), bf16[2,2,65536]{2,1,0:T(2,128)(2,1)S(1)}, u32[]{:S(2)}, u32[]{:S(2)}) async-start(bf16[2,2,65536]{2,1,0:T(2,128)(2,1)} %reshape.25), calls=%async_computation | async-start | bytes 1048576 | tf_op jit(solution)/shard_map/all_to_all | solution.py:62
  25.0 100.5 %all-gather.2.cloned.1.call-start = ((), (), s32[]{:S(2)}) async-start(), calls=%async_computation.1 | async-start | bytes 8912896 | tf_op jit(solution)/shard_map/all_gather | solution.py:66
  138.8 10.1 %copy-start = (bf16[8,256,1,1024]{1,0,3,2:T(8,128)(2,1)S(1)}, bf16[8,256,1,1024]{1,0,3,2:T(8,128)(2,1)}, u32[]{:S(2)}) copy-start(bf16[8,256,1,1024]{1,0,3,2:T(8,128)(2,1)} %copy.28) | copy-start | bytes 12582916
  138.8 10.1 %copy-start.8 = (bf16[4,16,2,2,1024]{1,0,3,4,2:T(4,128)(2,1)S(1)}, bf16[4,16,2,2,1024]{1,0,3,4,2:T(4,128)(2,1)}, u32[]{:S(2)}) copy-start(bf16[4,16,2,2,1024]{1,0,3,4,2:T(4,128)(2,1)} %copy.23) | copy-start | bytes 1572868
  163.0 5.3 %copy-start.5 = (bf16[8,256,1,1024]{1,0,3,2:T(8,128)(2,1)S(1)}, bf16[8,256,1,1024]{1,0,3,2:T(8,128)(2,1)}, u32[]{:S(2)}) copy-start(bf16[8,256,1,1024]{1,0,3,2:T(8,128)(2,1)} %copy.29) | copy-start | bytes 12582916
  212.2 9.1 %copy-start.1 = (bf16[8,256,1,1024]{1,0,3,2:T(8,128)(2,1)S(1)}, bf16[8,256,1,1024]{1,0,3,2:T(8,128)(2,1)}, u32[]{:S(2)}) copy-start(bf16[8,256,1,1024]{1,0,3,2:T(8,128)(2,1)} %copy.28) | copy-start | bytes 12582916
  271.0 10.2 %copy-start.2 = (bf16[8,256,1,1024]{1,0,3,2:T(8,128)(2,1)S(1)}, bf16[8,256,1,1024]{1,0,3,2:T(8,128)(2,1)}, u32[]{:S(2)}) copy-start(bf16[8,256,1,1024]{1,0,3,2:T(8,128)(2,1)} %copy.28) | copy-start | bytes 12582916
  271.0 10.2 %copy-start.9 = (bf16[4,16,2,2,1024]{1,0,3,4,2:T(4,128)(2,1)S(1)}, bf16[4,16,2,2,1024]{1,0,3,4,2:T(4,128)(2,1)}, u32[]{:S(2)}) copy-start(bf16[4,16,2,2,1024]{1,0,3,4,2:T(4,128)(2,1)} %copy.23) | copy-start | bytes 1572868
  281.2 6.9 %copy-start.6 = (bf16[8,256,1,1024]{1,0,3,2:T(8,128)(2,1)S(1)}, bf16[8,256,1,1024]{1,0,3,2:T(8,128)(2,1)}, u32[]{:S(2)}) copy-start(bf16[8,256,1,1024]{1,0,3,2:T(8,128)(2,1)} %copy.29) | copy-start | bytes 12582916
  332.8 9.0 %copy-start.3 = (bf16[8,256,1,1024]{1,0,3,2:T(8,128)(2,1)S(1)}, bf16[8,256,1,1024]{1,0,3,2:T(8,128)(2,1)}, u32[]{:S(2)}) copy-start(bf16[8,256,1,1024]{1,0,3,2:T(8,128)(2,1)} %copy.28) | copy-start | bytes 12582916
  393.9 10.0 %copy-start.4 = (bf16[8,256,1,1024]{1,0,3,2:T(8,128)(2,1)S(1)}, bf16[8,256,1,1024]{1,0,3,2:T(8,128)(2,1)}, u32[]{:S(2)}) copy-start(bf16[8,256,1,1024]{1,0,3,2:T(8,128)(2,1)} %copy.28) | copy-start | bytes 12582916
  393.9 10.0 %copy-start.10 = (bf16[4,16,2,2,1024]{1,0,3,4,2:T(4,128)(2,1)S(1)}, bf16[4,16,2,2,1024]{1,0,3,4,2:T(4,128)(2,1)}, u32[]{:S(2)}) copy-start(bf16[4,16,2,2,1024]{1,0,3,4,2:T(4,128)(2,1)} %copy.23) | copy-start | bytes 1572868
  403.9 6.9 %copy-start.7 = (bf16[8,256,1,1024]{1,0,3,2:T(8,128)(2,1)S(1)}, bf16[8,256,1,1024]{1,0,3,2:T(8,128)(2,1)}, u32[]{:S(2)}) copy-start(bf16[8,256,1,1024]{1,0,3,2:T(8,128)(2,1)} %copy.29) | copy-start | bytes 12582916
Sparse Core Ops, SparseCore 0:
  50.0 75.4 all-gather.1
where the time goes:
time: 492 us; the launch traced here: 487 us
  matrix products  200 us (41%)
  waiting for transfers between devices  80.5 us (16%)
  blocking collectives  79.4 us (16%)
  local copies, waits for them, and re-layouts  78.8 us (16%)
  other arithmetic  28.3 us (6%)
  between operations  15.1 us (3%)
    dot_general x20, matrix products, product(): return jnp.einsum(form, left, right, preferred_element_type=f32)  200 us
    psum x2, blocking collectives, solve_stack(): misfit = lax.psum(partial_misfit, ('win', 'chan'))  79.4 us
    all_gather x1, waiting for transfers between devices, body(): gathered = lax.all_gather(picked, 'chan', axis=1, tiled=True)  72.2 us
    unnamed x29, local copies, waits for them, and re-layouts  56.4 us
    another operation x1, other arithmetic, body(): stack = jnp.stack([gre, gim], axis=2)  13.7 us
    all_to_all x2, local copies, waits for them, and re-layouts, body(): lax.all_to_all(scaled, 'win', split_axis=3, concat_axis=0, tiled=True)  10.5 us
  transfers between devices with their start and end apart: 2, of which 2 were waited for; matrix products, arithmetic and copies ran while one was open for 1% of the time, Pallas kernels for 0%

commit v1 on v0

--- a/solution.py
+++ b/solution.py
@@ -63,7 +63,12 @@
     first = lax.axis_index("chan") * per_dev
     mine = lax.dynamic_slice_in_dim(order, first, per_dev, 0)
     picked = jnp.take(local, mine, axis=1)
-    gathered = lax.all_gather(picked, "chan", axis=1, tiled=True)
+    ring = [picked]
+    for hop in range(15):
+        ring.append(lax.ppermute(ring[-1], "chan", [(dev, (dev + 1) % 16) for dev in range(16)]))
+    gathered = jnp.roll(
+        jnp.concatenate(ring[::-1], axis=1), (lax.axis_index("chan") + 1) * ring[0].shape[1], axis=1
+    )
     gre, gim, weight = solve_stack(
         gathered[:, :, 0, :], gathered[:, :, 1, :], local[:, :, 0, :], local[:, :, 1, :], cells
     )

time: 492 us -> 594 us (1.21)
  waiting for transfers between devices: 80.5 us -> 175 us
  local copies, waits for them, and re-layouts: 78.8 us -> 95.7 us
  between operations: 15.1 us -> 2.04 us
    ppermute x0 -> x15, waiting for transfers between devices: none -> 166 us  [body(): lax.ppermute(ring[-1], 'chan', [(dev, (dev + 1) % 16) for dev in range(16)])]
    all_gather x1 -> x0, waiting for transfers between devices: 72.2 us -> none  [body(): gathered = lax.all_gather(picked, 'chan', axis=1, tiled=True)]
    squeeze x0 -> x2, local copies, waits for them, and re-layouts: none -> 14.6 us  [the longest x1 7.3 us: body(): gathered[:, :, 1, :]]
    unnamed x29 -> x98, local copies, waits for them, and re-layouts: 56.4 us -> 64.4 us
    slice x1 -> x0, local copies, waits for them, and re-layouts: 6 us -> none  [body(): gathered[:, :, 0, :]]
  transfers between devices with their start and end apart: 2 -> 16, of which waited for: 2 -> 16; matrix products, arithmetic and copies ran while one was open for 1% -> 1% of each run, Pallas kernels for 0% -> 0%
where the time goes in v1:
time: 594 us; the launch traced here: 586 us
  matrix products  203 us (34%)
  waiting for transfers between devices  175 us (29%)
  local copies, waits for them, and re-layouts  95.7 us (16%)
  blocking collectives  78 us (13%)
  other arithmetic  27.7 us (5%)
    dot_general x20, matrix products, product(): return jnp.einsum(form, left, right, preferred_element_type=f32)  203 us
    ppermute x15, waiting for transfers between devices, body(): lax.ppermute(ring[-1], 'chan', [(dev, (dev + 1) % 16) for dev in range(16)])  166 us
    psum x2, blocking collectives, solve_stack(): misfit = lax.psum(partial_misfit, ('win', 'chan'))  78 us
    unnamed x98, local copies, waits for them, and re-layouts  64.4 us
    another operation x1, other arithmetic, body(): stack = jnp.stack([gre, gim], axis=2)  13.8 us
  transfers between devices with their start and end apart: 16, of which 16 were waited for; matrix products, arithmetic and copies ran while one was open for 1% of the time, Pallas kernels for 0%

profile of v1, /device:TPU:0, one launch (start us, length us, event | category | flops | bytes accessed | tf_op | source)
XLA Modules:
  0.0 585.8 jit_solution(3956386419674077537)
XLA Ops:
  2.9 4.8 copy.93
  7.7 6.6 %reshape.25 = bf16[2,2,65536]{2,1,0:T(2,128)(2,1)} reshape(bf16[2048,2,4,16]{3,2,1,0:T(4,128)(2,1)} %bitcast.148) | data formatting | bytes 1048576
  14.3 4.2 all-to-all-start
  18.6 8.6 %all-to-all-done = bf16[2,2,65536]{2,1,0:T(2,128)(2,1)S(1)} async-done(((bf16[2,2,65536]{2,1,0:T(2,128)(2,1)}), bf16[2,2,65536]{2,1,0:T(2,128)(2,1)S(1)}, u32[]{:S(2)}, u32[]{:S(2)}) %all-to-all-start) | async-done | bytes 524320 | tf_op jit(solution)/shard_map/all_to_all | solution.py:62
  31.3 5.6 copy.94
  36.9 4.9 copy.95
  43.0 11.3 %collective-permute-done = bf16[8,16,2,1024]{3,1,2,0:T(8,128)(2,1)S(1)} collective-permute-done((bf16[8,16,2,1024]{3,1,2,0:T(8,128)(2,1)S(1)}, bf16[8,16,2,1024]{3,1,2,0:T(8,128)(2,1)S(1)}, u32[]{:S(2)}, u32[]{:S(2)}) %collective-permute-start) | collective-permute-done | bytes 524320 | tf_op jit(solution)/shard_map/ppermute | solution.py:68
  54.2 11.3 %collective-permute-done.1 = bf16[8,16,2,1024]{3,1,2,0:T(8,128)(2,1)S(1)} collective-permute-done((bf16[8,16,2,1024]{3,1,2,0:T(8,128)(2,1)S(1)}, bf16[8,16,2,1024]{3,1,2,0:T(8,128)(2,1)S(1)}, u32[]{:S(2)}, u32[]{:S(2)}) %collective-permute-start.1) | collective-permute-done | bytes 524320 | tf_op jit(solution)/shard_map/ppermute | solution.py:68
  65.5 11.3 %collective-permute-done.2 = bf16[8,16,2,1024]{3,1,2,0:T(8,128)(2,1)S(1)} collective-permute-done((bf16[8,16,2,1024]{3,1,2,0:T(8,128)(2,1)S(1)}, bf16[8,16,2,1024]{3,1,2,0:T(8,128)(2,1)S(1)}, u32[]{:S(2)}, u32[]{:S(2)}) %collective-permute-start.2) | collective-permute-done | bytes 524320 | tf_op jit(solution)/shard_map/ppermute | solution.py:68
  76.9 11.3 %collective-permute-done.3 = bf16[8,16,2,1024]{3,1,2,0:T(8,128)(2,1)S(1)} collective-permute-done((bf16[8,16,2,1024]{3,1,2,0:T(8,128)(2,1)S(1)}, bf16[8,16,2,1024]{3,1,2,0:T(8,128)(2,1)S(1)}, u32[]{:S(2)}, u32[]{:S(2)}) %collective-permute-start.3) | collective-permute-done | bytes 524320 | tf_op jit(solution)/shard_map/ppermute | solution.py:68
  88.2 11.3 %collective-permute-done.4 = bf16[8,16,2,1024]{3,1,2,0:T(8,128)(2,1)S(1)} collective-permute-done((bf16[8,16,2,1024]{3,1,2,0:T(8,128)(2,1)S(1)}, bf16[8,16,2,1024]{3,1,2,0:T(8,128)(2,1)S(1)}, u32[]{:S(2)}, u32[]{:S(2)}) %collective-permute-start.4) | collective-permute-done | bytes 524320 | tf_op jit(solution)/shard_map/ppermute | solution.py:68
  100.3 11.3 %collective-permute-done.5 = bf16[8,16,2,1024]{3,1,2,0:T(8,128)(2,1)S(1)} collective-permute-done((bf16[8,16,2,1024]{3,1,2,0:T(8,128)(2,1)S(1)}, bf16[8,16,2,1024]{3,1,2,0:T(8,128)(2,1)S(1)}, u32[]{:S(2)}, u32[]{:S(2)}) %collective-permute-start.5) | collective-permute-done | bytes 524320 | tf_op jit(solution)/shard_map/ppermute | solution.py:68
  112.4 11.3 %collective-permute-done.6 = bf16[8,16,2,1024]{3,1,2,0:T(8,128)(2,1)S(1)} collective-permute-done((bf16[8,16,2,1024]{3,1,2,0:T(8,128)(2,1)S(1)}, bf16[8,16,2,1024]{3,1,2,0:T(8,128)(2,1)S(1)}, u32[]{:S(2)}, u32[]{:S(2)}) %collective-permute-start.6) | collective-permute-done | bytes 524320 | tf_op jit(solution)/shard_map/ppermute | solution.py:68
  124.4 11.3 %collective-permute-done.7 = bf16[8,16,2,1024]{3,1,2,0:T(8,128)(2,1)S(1)} collective-permute-done((bf16[8,16,2,1024]{3,1,2,0:T(8,128)(2,1)S(1)}, bf16[8,16,2,1024]{3,1,2,0:T(8,128)(2,1)S(1)}, u32[]{:S(2)}, u32[]{:S(2)}) %collective-permute-start.7) | collective-permute-done | bytes 524320 | tf_op jit(solution)/shard_map/ppermute | solution.py:68
  136.5 11.3 %collective-permute-done.8 = bf16[8,16,2,1024]{3,1,2,0:T(8,128)(2,1)S(1)} collective-permute-done((bf16[8,16,2,1024]{3,1,2,0:T(8,128)(2,1)S(1)}, bf16[8,16,2,1024]{3,1,2,0:T(8,128)(2,1)S(1)}, u32[]{:S(2)}, u32[]{:S(2)}) %collective-permute-start.8) | collective-permute-done | bytes 524320 | tf_op jit(solution)/shard_map/ppermute | solution.py:68
  148.7 11.3 %collective-permute-done.9 = bf16[8,16,2,1024]{3,1,2,0:T(8,128)(2,1)S(1)} collective-permute-done((bf16[8,16,2,1024]{3,1,2,0:T(8,128)(2,1)S(1)}, bf16[8,16,2,1024]{3,1,2,0:T(8,128)(2,1)S(1)}, u32[]{:S(2)}, u32[]{:S(2)}) %collective-permute-start.9) | collective-permute-done | bytes 524320 | tf_op jit(solution)/shard_map/ppermute | solution.py:68
  160.8 11.3 %collective-permute-done.10 = bf16[8,16,2,1024]{3,1,2,0:T(8,128)(2,1)S(1)} collective-permute-done((bf16[8,16,2,1024]{3,1,2,0:T(8,128)(2,1)S(1)}, bf16[8,16,2,1024]{3,1,2,0:T(8,128)(2,1)S(1)}, u32[]{:S(2)}, u32[]{:S(2)}) %collective-permute-start.10) | collective-permute-done | bytes 524320 | tf_op jit(solution)/shard_map/ppermute | solution.py:68
  172.9 11.3 %collective-permute-done.11 = bf16[8,16,2,1024]{3,1,2,0:T(8,128)(2,1)S(1)} collective-permute-done((bf16[8,16,2,1024]{3,1,2,0:T(8,128)(2,1)S(1)}, bf16[8,16,2,1024]{3,1,2,0:T(8,128)(2,1)S(1)}, u32[]{:S(2)}, u32[]{:S(2)}) %collective-permute-start.11) | collective-permute-done | bytes 524320 | tf_op jit(solution)/shard_map/ppermute | solution.py:68
  185.0 11.3 %collective-permute-done.12 = bf16[8,16,2,1024]{3,1,2,0:T(8,128)(2,1)S(1)} collective-permute-done((bf16[8,16,2,1024]{3,1,2,0:T(8,128)(2,1)S(1)}, bf16[8,16,2,1024]{3,1,2,0:T(8,128)(2,1)S(1)}, u32[]{:S(2)}, u32[]{:S(2)}) %collective-permute-start.12) | collective-permute-done | bytes 524320 | tf_op jit(solution)/shard_map/ppermute | solution.py:68
  197.1 11.4 %collective-permute-done.13 = bf16[8,16,2,1024]{3,1,2,0:T(8,128)(2,1)} collective-permute-done((bf16[8,16,2,1024]{3,1,2,0:T(8,128)(2,1)S(1)}, bf16[8,16,2,1024]{3,1,2,0:T(8,128)(2,1)}, u32[]{:S(2)}, u32[]{:S(2)}) %collective-permute-start.13) | collective-permute-done | bytes 524320 | tf_op jit(solution)/shard_map/ppermute | solution.py:68
  212.3 7.9 %collective-permute-done.14 = bf16[8,16,2,1024]{3,1,2,0:T(8,128)(2,1)} collective-permute-done((bf16[8,16,2,1024]{3,1,2,0:T(8,128)(2,1)}, bf16[8,16,2,1024]{3,1,2,0:T(8,128)(2,1)}, u32[]{:S(2)}, u32[]{:S(2)}) %collective-permute-start.14) | collective-permute-done | bytes 524320 | tf_op jit(solution)/shard_map/ppermute | solution.py:68
  236.0 5.0 add_reduce_fusion.2
  241.0 7.3 %copy.129 = bf16[8,256,1024]{1,0,2:T(8,128)(2,1)} copy(bf16[8,256,1024]{2,0,1:T(8,128)(2,1)} %get-tuple-element.13) | data formatting | bytes 8388608 | tf_op jit(solution)/shard_map/squeeze | solution.py:73
  248.3 10.0 %fusion.44 = f32[1024,16,256]{2,1,0:T(8,128)} fusion(bf16[8,256,1024]{1,0,2:T(8,128)(2,1)} %copy.129, bf16[8,16,2,1024]{1,0,3,2:T(8,128)(2,1)} %bitcast.134), kind=kOutput, calls=%fused_computation.90 | convolution fusion | flops 67108864 | bytes 23068672 | tf_op jit(solution)/shard_map/ksf,kcf->scf/dot_general | solution.py:25
  258.2 6.7 %fusion.45 = f32[1024,16,256]{2,1,0:T(8,128)} fusion(bf16[8,256,1024]{1,0,2:T(8,128)(2,1)S(1)} %copy-done, bf16[8,16,2,1024]{1,0,3,2:T(8,128)(2,1)S(1)} %bitcast.142), kind=kOutput, calls=%fused_computation.91 | convolution fusion | flops 67108864 | bytes 23068672 | tf_op jit(solution)/shard_map/ksf,kcf->scf/dot_general | solution.py:25
  265.0 7.3 %copy.130 = bf16[8,256,1024]{1,0,2:T(8,128)(2,1)} copy(bf16[8,256,1024]{2,0,1:T(8,128)(2,1)} %get-tuple-element.14) | data formatting | bytes 8388608 | tf_op jit(solution)/shard_map/squeeze | solution.py:73
  272.3 12.6 %multiply_convert_fusion.1 = bf16[1024,16,256]{2,1,0:T(8,128)(2,1)} fusion(f32[1024,16,256]{2,1,0:T(8,128)} %fusion.44, bf16[8,256,1024]{1,0,2:T(8,128)(2,1)} %copy.130, bf16[8,16,2,1024]{1,0,3,2:T(8,128)(2,1)} %bitcast.135), kind=kOutput, calls=%fused_computation.9 | convolution fusion | flops 79691776 | bytes 31457280 | tf_op jit(solution)/shard_map/ksf,kcf->scf/dot_general | solution.py:25
  284.9 7.7 %fusion.12 = f32[1024,16,8]{1,2,0:T(8,128)} fusion(bf16[8,256,1024]{1,0,2:T(8,128)(2,1)S(1)} %copy-done.7, bf16[1024,16,256]{2,1,0:T(8,128)(2,1)} %multiply_convert_fusion.1), kind=kOutput, calls=%fused_computation.22 | convolution fusion | flops 67108864 | bytes 13107200 | tf_op jit(solution)/shard_map/ksf,scf->kcf/dot_general | solution.py:25
  292.6 16.6 %add_reduce_fusion.1 = (f32[]{:T(128)}, bf16[1024,16,256]{2,1,0:T(8,128)(2,1)}) fusion(bf16[1024,16,256]{2,1,0:T(8,128)(2,1)} %multiply_convert_fusion.1, f32[1024,16,256]{2,1,0:T(8,128)} %fusion.45, bf16[8,256,1024]{1,0,2:T(8,128)(2,1)} %copy.130, bf16[8,16,2,1024]{1,0,3,2:T(8,128)(2,1)} %bitcast.136), kind=kOutput, calls=%fused_computation.7 | convolution fusion | flops 104857600 | bytes 39845892 | tf_op jit(solution)/shard_map/ksf,kcf->scf/dot_general | solution.py:25
  309.1 8.9 %fusion.8 = f32[1024,16,8]{1,2,0:T(8,128)} fusion(bf16[8,256,1024]{1,0,2:T(8,128)(2,1)} %copy.129, bf16[1024,16,256]{2,1,0:T(8,128)(2,1)} %get-tuple-element.22), kind=kOutput, calls=%fused_computation.18 | convolution fusion | flops 67108864 | bytes 13107200 | tf_op jit(solution)/shard_map/ksf,scf->kcf/dot_general | solution.py:25
  318.1 7.7 %fusion.10 = f32[1024,16,8]{1,2,0:T(8,128)} fusion(bf16[8,256,1024]{1,0,2:T(8,128)(2,1)S(1)} %copy-done.8, bf16[1024,16,256]{2,1,0:T(8,128)(2,1)} %get-tuple-element.22), kind=kOutput, calls=%fused_computation.20 | convolution fusion | flops 67108864 | bytes 13107200 | tf_op jit(solution)/shard_map/ksf,scf->kcf/dot_general | solution.py:25
  326.2 10.7 %fusion.21 = f32[8]{0:T(128)S(1)} fusion(f32[1024,16,8]{1,2,0:T(8,128)} %fusion.8, f32[1024,16,8]{1,2,0:T(8,128)} %fusion.12, f32[1024,16,8]{1,2,0:T(8,128)} %fusion.10, bf16[8,256,1024]{1,0,2:T(8,128)(2,1)} %copy.129, bf16[1024,16,256]{2,1,0:T(8,128)(2,1)} %multiply_convert_fusion.1, bf16[8,16,2,1024]{1,0,3,2:T(8,128)(2,1)} %bitcast.137), kind=kOutput, calls=%fused_computation.42 | convolution fusion | flops 68157432 | bytes 14680096 | tf_op jit(solution)/shard_map/ksf,scf->kcf/dot_general | solution.py:25
  337.5 37.1 %psum.14 = f32[8]{0:T(128)S(1)} all-reduce(f32[8]{0:T(128)S(1)} %subtract_add_fusion.1), channel_id=1, replica_groups=mesh['win'=2,'chan'=16] {'win','chan'}, use_global_device_ids=true, to_apply=%region_5.6 | all-reduce | flops 8 | bytes 64 | tf_op jit(solution)/shard_map/psum | solution.py:44
  375.2 10.1 %fusion.42 = f32[1024,16,256]{2,1,0:T(8,128)} fusion(bf16[8,256,1024]{1,0,2:T(8,128)(2,1)} %copy.129, f32[8]{0:T(128)S(1)} %get-tuple-element.20, bf16[8,16,2,1024]{1,0,3,2:T(8,128)(2,1)} %bitcast.138), kind=kOutput, calls=%fused_computation.57 | convolution fusion | flops 67502080 | bytes 23068704 | tf_op jit(solution)/shard_map/ksf,kcf->scf/dot_general | solution.py:25
  385.3 6.9 %fusion.35 = f32[1024,16,256]{2,1,0:T(8,128)} fusion(bf16[8,256,1024]{1,0,2:T(8,128)(2,1)S(1)} %copy-done.1, f32[8]{0:T(128)S(1)} %get-tuple-element.20, bf16[8,16,2,1024]{1,0,3,2:T(8,128)(2,1)S(1)} %bitcast.143), kind=kOutput, calls=%fused_computation.55 | convolution fusion | flops 67502080 | bytes 23069184 | tf_op jit(solution)/shard_map/ksf,kcf->scf/dot_general | solution.py:25
  392.2 11.9 %divide_convert_fusion.3 = bf16[1024,16,256]{2,1,0:T(8,128)(2,1)} fusion(f32[1024,16,256]{2,1,0:T(8,128)} %fusion.42, bf16[8,256,1024]{1,0,2:T(8,128)(2,1)S(1)} %copy-done.9, f32[]{:T(128)} %get-tuple-element.19, f32[8]{0:T(128)S(1)} %get-tuple-element.20, bf16[8,16,2,1024]{1,0,3,2:T(8,128)(2,1)S(1)} %bitcast.144), kind=kOutput, calls=%fused_computation.6 | convolution fusion | flops 80084992 | bytes 31457796 | tf_op jit(solution)/shard_map/ksf,kcf->scf/dot_general | solution.py:25
  404.0 7.7 %fusion.4 = f32[1024,16,8]{1,2,0:T(8,128)} fusion(bf16[8,256,1024]{1,0,2:T(8,128)(2,1)S(1)} %copy-done.9, bf16[1024,16,256]{2,1,0:T(8,128)(2,1)} %divide_convert_fusion.3), kind=kOutput, calls=%fused_computation.14 | convolution fusion | flops 67108864 | bytes 13107200 | tf_op jit(solution)/shard_map/ksf,scf->kcf/dot_general | solution.py:25
  411.7 17.4 %add_reduce_fusion = (f32[]{:T(128)}, bf16[1024,16,256]{2,1,0:T(8,128)(2,1)}) fusion(bf16[1024,16,256]{2,1,0:T(8,128)(2,1)} %divide_convert_fusion.3, f32[]{:T(128)} %get-tuple-element.19, f32[1024,16,256]{2,1,0:T(8,128)} %fusion.35, bf16[8,256,1024]{1,0,2:T(8,128)(2,1)} %copy.130, f32[8]{0:T(128)S(1)} %get-tuple-element.20, ...), kind=kOutput, calls=%fused_computation.4 | convolution fusion | flops 105250816 | bytes 39846436 | tf_op jit(solution)/shard_map/ksf,kcf->scf/dot_general | solution.py:25
  429.1 8.8 %fusion = f32[1024,16,8]{1,2,0:T(8,128)} fusion(bf16[8,256,1024]{1,0,2:T(8,128)(2,1)} %copy.129, bf16[1024,16,256]{2,1,0:T(8,128)(2,1)} %get-tuple-element.24), kind=kOutput, calls=%fused_computation.10 | convolution fusion | flops 67108864 | bytes 13107200 | tf_op jit(solution)/shard_map/ksf,scf->kcf/dot_general | solution.py:25
  437.9 9.0 %fusion.2 = f32[1024,16,8]{1,2,0:T(8,128)} fusion(bf16[8,256,1024]{1,0,2:T(8,128)(2,1)} %copy.130, bf16[1024,16,256]{2,1,0:T(8,128)(2,1)} %get-tuple-element.24), kind=kOutput, calls=%fused_computation.12 | convolution fusion | flops 67108864 | bytes 13107200 | tf_op jit(solution)/shard_map/ksf,scf->kcf/dot_general | solution.py:25
  446.9 9.9 %fusion.24 = f32[8]{0:T(128)S(1)} fusion(f32[1024,16,8]{1,2,0:T(8,128)} %fusion, f32[1024,16,8]{1,2,0:T(8,128)} %fusion.4, f32[1024,16,8]{1,2,0:T(8,128)} %fusion.2, bf16[8,256,1024]{1,0,2:T(8,128)(2,1)S(1)} %copy-done.2, bf16[1024,16,256]{2,1,0:T(8,128)(2,1)} %divide_convert_fusion.3, bf16[8,16,2,1024]{1,0,3,2:T(8,128)(2,1)} %bitcast.140), kind=kOutput, calls=%fused_computation.45 | convolution fusion | flops 68157432 | bytes 14680096 | tf_op jit(solution)/shard_map/ksf,scf->kcf/dot_general | solution.py:25
  457.4 41.0 %psum.15 = f32[8]{0:T(128)S(1)} all-reduce(f32[8]{0:T(128)S(1)} %subtract_add_fusion), channel_id=1, replica_groups=mesh['win'=2,'chan'=16] {'win','chan'}, use_global_device_ids=true, to_apply=%region_9.10 | all-reduce | flops 8 | bytes 64 | tf_op jit(solution)/shard_map/psum | solution.py:44
  499.7 9.9 %fusion.32 = f32[1024,16,256]{2,1,0:T(8,128)} fusion(bf16[8,256,1024]{1,0,2:T(8,128)(2,1)} %copy.129, f32[8]{0:T(128)S(1)} %get-tuple-element.18, bf16[8,16,2,1024]{1,0,3,2:T(8,128)(2,1)} %bitcast.141), kind=kOutput, calls=%fused_computation.54 | convolution fusion | flops 67502080 | bytes 23068704 | tf_op jit(solution)/shard_map/ksf,kcf->scf/dot_general | solution.py:25
  509.6 6.9 %fusion.39 = f32[1024,16,256]{2,1,0:T(8,128)} fusion(bf16[8,256,1024]{1,0,2:T(8,128)(2,1)S(1)} %copy-done.3, f32[8]{0:T(128)S(1)} %get-tuple-element.18, bf16[8,16,2,1024]{1,0,3,2:T(8,128)(2,1)S(1)} %bitcast.145), kind=kOutput, calls=%fused_computation.56 | convolution fusion | flops 67502080 | bytes 23069184 | tf_op jit(solution)/shard_map/ksf,kcf->scf/dot_general | solution.py:25
  516.5 11.9 %fusion.17 = bf16[256,16,1,1024]{0,1,3,2:T(8,128)(2,1)} fusion(f32[]{:T(128)} %fusion.47, f32[1024,16,256]{2,1,0:T(8,128)} %fusion.32, bf16[8,256,1024]{1,0,2:T(8,128)(2,1)S(1)} %copy-done.10, f32[8]{0:T(128)S(1)} %get-tuple-element.18, bf16[8,16,2,1024]{1,0,3,2:T(8,128)(2,1)S(1)} %bitcast.146), kind=kOutput, calls=%fused_computation.38 | convolution fusion | flops 80084992 | bytes 31457796 | tf_op jit(solution)/shard_map/ksf,kcf->scf/dot_general | solution.py:25
  528.4 11.8 %fusion.16 = bf16[256,16,1,1024]{0,1,3,2:T(8,128)(2,1)} fusion(f32[]{:T(128)} %fusion.47, f32[1024,16,256]{2,1,0:T(8,128)} %fusion.39, bf16[8,256,1024]{1,0,2:T(8,128)(2,1)S(1)} %copy-done.10, f32[8]{0:T(128)S(1)} %get-tuple-element.18, bf16[8,16,2,1024]{1,0,3,2:T(8,128)(2,1)S(1)} %bitcast.147), kind=kOutput, calls=%fused_computation.37 | convolution fusion | flops 80084992 | bytes 31457796 | tf_op jit(solution)/shard_map/ksf,kcf->scf/dot_general | solution.py:25
  540.2 13.8 %pad_maximum_fusion = bf16[256,16,2,1024]{0,1,3,2:T(8,128)(2,1)} fusion(bf16[256,16,1,1024]{0,1,3,2:T(8,128)(2,1)} %fusion.17, bf16[256,16,1,1024]{0,1,3,2:T(8,128)(2,1)} %fusion.16), kind=kLoop, calls=%fused_computation.1 | loop fusion | flops 8388608 | bytes 33554432 | tf_op jit(solution)/shard_map/stack | solution.py:75
  554.0 31.0 %copy.149 = bf16[256,16,2,1024]{3,2,1,0:T(2,128)(2,1)} copy(bf16[256,16,2,1024]{0,1,3,2:T(8,128)(2,1)} %pad_maximum_fusion) | data formatting | bytes 33554432
  (128 shorter events, 37.5 us)
Async XLA Ops:
  0.6 17.9 %copy-start.31 = (s32[256]{0:T(256)S(1)}, s32[256]{0:T(256)}, u32[]{:S(2)}) copy-start(s32[256]{0:T(256)} %param.7) | copy-start | bytes 3076
  14.3 12.9 %all-to-all-start = ((bf16[2,2,65536]{2,1,0:T(2,128)(2,1)}), bf16[2,2,65536]{2,1,0:T(2,128)(2,1)S(1)}, u32[]{:S(2)}, u32[]{:S(2)}) async-start(bf16[2,2,65536]{2,1,0:T(2,128)(2,1)} %reshape.25), calls=%async_computation | async-start | bytes 1048576 | tf_op jit(solution)/shard_map/all_to_all | solution.py:62
  42.9 11.4 %collective-permute-start = (bf16[8,16,2,1024]{3,1,2,0:T(8,128)(2,1)S(1)}, bf16[8,16,2,1024]{3,1,2,0:T(8,128)(2,1)S(1)}, u32[]{:S(2)}, u32[]{:S(2)}) collective-permute-start(bf16[8,16,2,1024]{3,1,2,0:T(8,128)(2,1)S(1)} %copy.96), channel_id=1, source_target_pairs={{0,1},{1,2},{2,3},{3,4},{4,5},{5,6},{6,7},{7,8},{8,9},{9,10},{10,1... | collective-permute-start | bytes 1572872 | tf_op jit(solution)/shard_map/ppermute | solution.py:68
  54.2 11.3 %collective-permute-start.1 = (bf16[8,16,2,1024]{3,1,2,0:T(8,128)(2,1)S(1)}, bf16[8,16,2,1024]{3,1,2,0:T(8,128)(2,1)S(1)}, u32[]{:S(2)}, u32[]{:S(2)}) collective-permute-start(bf16[8,16,2,1024]{3,1,2,0:T(8,128)(2,1)S(1)} %collective-permute-done), channel_id=1, source_target_pairs={{0,1},{1,2},{2,3},{3,4},{4,5},{5,6},{6,7},{7,8},{8,9},{9,10},{10,1... | collective-permute-start | bytes 1572872 | tf_op jit(solution)/shard_map/ppermute | solution.py:68
  65.5 11.3 %collective-permute-start.2 = (bf16[8,16,2,1024]{3,1,2,0:T(8,128)(2,1)S(1)}, bf16[8,16,2,1024]{3,1,2,0:T(8,128)(2,1)S(1)}, u32[]{:S(2)}, u32[]{:S(2)}) collective-permute-start(bf16[8,16,2,1024]{3,1,2,0:T(8,128)(2,1)S(1)} %collective-permute-done.1), channel_id=1, source_target_pairs={{0,1},{1,2},{2,3},{3,4},{4,5},{5,6},{6,7},{7,8},{8,9},{9,10},{10,1... | collective-permute-start | bytes 1572872 | tf_op jit(solution)/shard_map/ppermute | solution.py:68
  76.8 11.3 %collective-permute-start.3 = (bf16[8,16,2,1024]{3,1,2,0:T(8,128)(2,1)S(1)}, bf16[8,16,2,1024]{3,1,2,0:T(8,128)(2,1)S(1)}, u32[]{:S(2)}, u32[]{:S(2)}) collective-permute-start(bf16[8,16,2,1024]{3,1,2,0:T(8,128)(2,1)S(1)} %collective-permute-done.2), channel_id=1, source_target_pairs={{0,1},{1,2},{2,3},{3,4},{4,5},{5,6},{6,7},{7,8},{8,9},{9,10},{10,1... | collective-permute-start | bytes 1572872 | tf_op jit(solution)/shard_map/ppermute | solution.py:68
  88.2 120.5 %copy-start.11 = (bf16[8,16,2,1024]{3,1,2,0:T(8,128)(2,1)}, bf16[8,16,2,1024]{3,1,2,0:T(8,128)(2,1)S(1)}, u32[]{:S(2)}) copy-start(bf16[8,16,2,1024]{3,1,2,0:T(8,128)(2,1)S(1)} %collective-permute-done.3) | copy-start | bytes 1572868
  88.2 11.3 %collective-permute-start.4 = (bf16[8,16,2,1024]{3,1,2,0:T(8,128)(2,1)S(1)}, bf16[8,16,2,1024]{3,1,2,0:T(8,128)(2,1)S(1)}, u32[]{:S(2)}, u32[]{:S(2)}) collective-permute-start(bf16[8,16,2,1024]{3,1,2,0:T(8,128)(2,1)S(1)} %collective-permute-done.3), channel_id=1, source_target_pairs={{0,1},{1,2},{2,3},{3,4},{4,5},{5,6},{6,7},{7,8},{8,9},{9,10},{10,1... | collective-permute-start | bytes 1572872 | tf_op jit(solution)/shard_map/ppermute | solution.py:68
  99.5 0.8 copy-start.13
  100.3 11.3 %collective-permute-start.5 = (bf16[8,16,2,1024]{3,1,2,0:T(8,128)(2,1)S(1)}, bf16[8,16,2,1024]{3,1,2,0:T(8,128)(2,1)S(1)}, u32[]{:S(2)}, u32[]{:S(2)}) collective-permute-start(bf16[8,16,2,1024]{3,1,2,0:T(8,128)(2,1)S(1)} %collective-permute-done.4), channel_id=1, source_target_pairs={{0,1},{1,2},{2,3},{3,4},{4,5},{5,6},{6,7},{7,8},{8,9},{9,10},{10,1... | collective-permute-start | bytes 1572872 | tf_op jit(solution)/shard_map/ppermute | solution.py:68
  111.6 0.8 copy-start.15
  112.4 11.3 %collective-permute-start.6 = (bf16[8,16,2,1024]{3,1,2,0:T(8,128)(2,1)S(1)}, bf16[8,16,2,1024]{3,1,2,0:T(8,128)(2,1)S(1)}, u32[]{:S(2)}, u32[]{:S(2)}) collective-permute-start(bf16[8,16,2,1024]{3,1,2,0:T(8,128)(2,1)S(1)} %collective-permute-done.5), channel_id=1, source_target_pairs={{0,1},{1,2},{2,3},{3,4},{4,5},{5,6},{6,7},{7,8},{8,9},{9,10},{10,1... | collective-permute-start | bytes 1572872 | tf_op jit(solution)/shard_map/ppermute | solution.py:68
  123.7 0.8 copy-start.17
  124.4 11.3 %collective-permute-start.7 = (bf16[8,16,2,1024]{3,1,2,0:T(8,128)(2,1)S(1)}, bf16[8,16,2,1024]{3,1,2,0:T(8,128)(2,1)S(1)}, u32[]{:S(2)}, u32[]{:S(2)}) collective-permute-start(bf16[8,16,2,1024]{3,1,2,0:T(8,128)(2,1)S(1)} %collective-permute-done.6), channel_id=1, source_target_pairs={{0,1},{1,2},{2,3},{3,4},{4,5},{5,6},{6,7},{7,8},{8,9},{9,10},{10,1... | collective-permute-start | bytes 1572872 | tf_op jit(solution)/shard_map/ppermute | solution.py:68
  135.7 0.8 copy-start.19
  136.5 11.3 %collective-permute-start.8 = (bf16[8,16,2,1024]{3,1,2,0:T(8,128)(2,1)S(1)}, bf16[8,16,2,1024]{3,1,2,0:T(8,128)(2,1)S(1)}, u32[]{:S(2)}, u32[]{:S(2)}) collective-permute-start(bf16[8,16,2,1024]{3,1,2,0:T(8,128)(2,1)S(1)} %collective-permute-done.7), channel_id=1, source_target_pairs={{0,1},{1,2},{2,3},{3,4},{4,5},{5,6},{6,7},{7,8},{8,9},{9,10},{10,1... | collective-permute-start | bytes 1572872 | tf_op jit(solution)/shard_map/ppermute | solution.py:68
  147.8 0.8 copy-start.21
  148.7 11.3 %collective-permute-start.9 = (bf16[8,16,2,1024]{3,1,2,0:T(8,128)(2,1)S(1)}, bf16[8,16,2,1024]{3,1,2,0:T(8,128)(2,1)S(1)}, u32[]{:S(2)}, u32[]{:S(2)}) collective-permute-start(bf16[8,16,2,1024]{3,1,2,0:T(8,128)(2,1)S(1)} %collective-permute-done.8), channel_id=1, source_target_pairs={{0,1},{1,2},{2,3},{3,4},{4,5},{5,6},{6,7},{7,8},{8,9},{9,10},{10,1... | collective-permute-start | bytes 1572872 | tf_op jit(solution)/shard_map/ppermute | solution.py:68
  160.0 0.8 copy-start.23
  160.7 11.3 %collective-permute-start.10 = (bf16[8,16,2,1024]{3,1,2,0:T(8,128)(2,1)S(1)}, bf16[8,16,2,1024]{3,1,2,0:T(8,128)(2,1)S(1)}, u32[]{:S(2)}, u32[]{:S(2)}) collective-permute-start(bf16[8,16,2,1024]{3,1,2,0:T(8,128)(2,1)S(1)} %collective-permute-done.9), channel_id=1, source_target_pairs={{0,1},{1,2},{2,3},{3,4},{4,5},{5,6},{6,7},{7,8},{8,9},{9,10},{10,1... | collective-permute-start | bytes 1572872 | tf_op jit(solution)/shard_map/ppermute | solution.py:68
  172.1 0.8 copy-start.25
  172.8 11.3 %collective-permute-start.11 = (bf16[8,16,2,1024]{3,1,2,0:T(8,128)(2,1)S(1)}, bf16[8,16,2,1024]{3,1,2,0:T(8,128)(2,1)S(1)}, u32[]{:S(2)}, u32[]{:S(2)}) collective-permute-start(bf16[8,16,2,1024]{3,1,2,0:T(8,128)(2,1)S(1)} %collective-permute-done.10), channel_id=1, source_target_pairs={{0,1},{1,2},{2,3},{3,4},{4,5},{5,6},{6,7},{7,8},{8,9},{9,10},{10,1... | collective-permute-start | bytes 1572872 | tf_op jit(solution)/shard_map/ppermute | solution.py:68
  184.2 0.8 copy-start.27
  185.0 11.3 %collective-permute-start.12 = (bf16[8,16,2,1024]{3,1,2,0:T(8,128)(2,1)S(1)}, bf16[8,16,2,1024]{3,1,2,0:T(8,128)(2,1)S(1)}, u32[]{:S(2)}, u32[]{:S(2)}) collective-permute-start(bf16[8,16,2,1024]{3,1,2,0:T(8,128)(2,1)S(1)} %collective-permute-done.11), channel_id=1, source_target_pairs={{0,1},{1,2},{2,3},{3,4},{4,5},{5,6},{6,7},{7,8},{8,9},{9,10},{10,1... | collective-permute-start | bytes 1572872 | tf_op jit(solution)/shard_map/ppermute | solution.py:68
  196.3 0.8 copy-start.29
  197.1 11.4 %collective-permute-start.13 = (bf16[8,16,2,1024]{3,1,2,0:T(8,128)(2,1)S(1)}, bf16[8,16,2,1024]{3,1,2,0:T(8,128)(2,1)}, u32[]{:S(2)}, u32[]{:S(2)}) collective-permute-start(bf16[8,16,2,1024]{3,1,2,0:T(8,128)(2,1)S(1)} %collective-permute-done.12), channel_id=1, source_target_pairs={{0,1},{1,2},{2,3},{3,4},{4,5},{5,6},{6,7},{7,8},{8,9},{9,10},{10,1... | collective-permute-start | bytes 1572872 | tf_op jit(solution)/shard_map/ppermute | solution.py:68
  208.5 11.8 %collective-permute-start.14 = (bf16[8,16,2,1024]{3,1,2,0:T(8,128)(2,1)}, bf16[8,16,2,1024]{3,1,2,0:T(8,128)(2,1)}, u32[]{:S(2)}, u32[]{:S(2)}) collective-permute-start(bf16[8,16,2,1024]{3,1,2,0:T(8,128)(2,1)} %collective-permute-done.13), channel_id=1, source_target_pairs={{0,1},{1,2},{2,3},{3,4},{4,5},{5,6},{6,7},{7,8},{8,9},{9,10},{10,1... | collective-permute-start | bytes 1572872 | tf_op jit(solution)/shard_map/ppermute | solution.py:68
  208.7 17.1 %copy-start.26 = (bf16[8,16,2,1024]{3,1,2,0:T(8,128)(2,1)S(1)}, bf16[8,16,2,1024]{3,1,2,0:T(8,128)(2,1)}, u32[]{:S(2)}) copy-start(bf16[8,16,2,1024]{3,1,2,0:T(8,128)(2,1)} %copy-done.25) | copy-start | bytes 1572868
  208.7 17.4 %copy-start.24 = (bf16[8,16,2,1024]{3,1,2,0:T(8,128)(2,1)S(1)}, bf16[8,16,2,1024]{3,1,2,0:T(8,128)(2,1)}, u32[]{:S(2)}) copy-start(bf16[8,16,2,1024]{3,1,2,0:T(8,128)(2,1)} %copy-done.23) | copy-start | bytes 1572868
  208.7 17.7 %copy-start.22 = (bf16[8,16,2,1024]{3,1,2,0:T(8,128)(2,1)S(1)}, bf16[8,16,2,1024]{3,1,2,0:T(8,128)(2,1)}, u32[]{:S(2)}) copy-start(bf16[8,16,2,1024]{3,1,2,0:T(8,128)(2,1)} %copy-done.21) | copy-start | bytes 1572868
  208.7 18.0 %copy-start.20 = (bf16[8,16,2,1024]{3,1,2,0:T(8,128)(2,1)S(1)}, bf16[8,16,2,1024]{3,1,2,0:T(8,128)(2,1)}, u32[]{:S(2)}) copy-start(bf16[8,16,2,1024]{3,1,2,0:T(8,128)(2,1)} %copy-done.19) | copy-start | bytes 1572868
  208.7 18.3 %copy-start.18 = (bf16[8,16,2,1024]{3,1,2,0:T(8,128)(2,1)S(1)}, bf16[8,16,2,1024]{3,1,2,0:T(8,128)(2,1)}, u32[]{:S(2)}) copy-start(bf16[8,16,2,1024]{3,1,2,0:T(8,128)(2,1)} %copy-done.17) | copy-start | bytes 1572868
  208.7 18.6 %copy-start.16 = (bf16[8,16,2,1024]{3,1,2,0:T(8,128)(2,1)S(1)}, bf16[8,16,2,1024]{3,1,2,0:T(8,128)(2,1)}, u32[]{:S(2)}) copy-start(bf16[8,16,2,1024]{3,1,2,0:T(8,128)(2,1)} %copy-done.15) | copy-start | bytes 1572868
  208.7 18.9 %copy-start.14 = (bf16[8,16,2,1024]{3,1,2,0:T(8,128)(2,1)S(1)}, bf16[8,16,2,1024]{3,1,2,0:T(8,128)(2,1)}, u32[]{:S(2)}) copy-start(bf16[8,16,2,1024]{3,1,2,0:T(8,128)(2,1)} %copy-done.13) | copy-start | bytes 1572868
  208.7 19.2 %copy-start.12 = (bf16[8,16,2,1024]{3,1,2,0:T(8,128)(2,1)S(1)}, bf16[8,16,2,1024]{3,1,2,0:T(8,128)(2,1)}, u32[]{:S(2)}) copy-start(bf16[8,16,2,1024]{3,1,2,0:T(8,128)(2,1)} %copy-done.11) | copy-start | bytes 1572868
  222.9 9.0 %copy-start.30 = (bf16[8,16,2,1024]{3,1,2,0:T(8,128)(2,1)S(1)}, bf16[8,16,2,1024]{3,1,2,0:T(8,128)(2,1)}, u32[]{:S(2)}) copy-start(bf16[8,16,2,1024]{3,1,2,0:T(8,128)(2,1)} %copy-done.29) | copy-start | bytes 1572868
  224.3 7.9 %copy-start.28 = (bf16[8,16,2,1024]{3,1,2,0:T(8,128)(2,1)S(1)}, bf16[8,16,2,1024]{3,1,2,0:T(8,128)(2,1)}, u32[]{:S(2)}) copy-start(bf16[8,16,2,1024]{3,1,2,0:T(8,128)(2,1)} %copy-done.27) | copy-start | bytes 1572868
  248.3 10.0 %copy-start = (bf16[8,256,1024]{1,0,2:T(8,128)(2,1)S(1)}, bf16[8,256,1024]{1,0,2:T(8,128)(2,1)}, u32[]{:S(2)}) copy-start(bf16[8,256,1024]{1,0,2:T(8,128)(2,1)} %copy.129) | copy-start | bytes 12582916
  248.3 10.0 %copy-start.4 = (bf16[4,16,2,2,1024]{1,0,3,4,2:T(4,128)(2,1)S(1)}, bf16[4,16,2,2,1024]{1,0,3,4,2:T(4,128)(2,1)}, u32[]{:S(2)}) copy-start(bf16[4,16,2,2,1024]{1,0,3,4,2:T(4,128)(2,1)} %copy.94) | copy-start | bytes 1572868
  272.3 12.6 %copy-start.7 = (bf16[8,256,1024]{1,0,2:T(8,128)(2,1)S(1)}, bf16[8,256,1024]{1,0,2:T(8,128)(2,1)}, u32[]{:S(2)}) copy-start(bf16[8,256,1024]{1,0,2:T(8,128)(2,1)} %copy.130) | copy-start | bytes 12582916
  309.1 8.9 %copy-start.8 = (bf16[8,256,1024]{1,0,2:T(8,128)(2,1)S(1)}, bf16[8,256,1024]{1,0,2:T(8,128)(2,1)}, u32[]{:S(2)}) copy-start(bf16[8,256,1024]{1,0,2:T(8,128)(2,1)} %copy.130) | copy-start | bytes 12582916
  375.2 10.1 %copy-start.1 = (bf16[8,256,1024]{1,0,2:T(8,128)(2,1)S(1)}, bf16[8,256,1024]{1,0,2:T(8,128)(2,1)}, u32[]{:S(2)}) copy-start(bf16[8,256,1024]{1,0,2:T(8,128)(2,1)} %copy.129) | copy-start | bytes 12582916
  375.2 10.1 %copy-start.5 = (bf16[4,16,2,2,1024]{1,0,3,4,2:T(4,128)(2,1)S(1)}, bf16[4,16,2,2,1024]{1,0,3,4,2:T(4,128)(2,1)}, u32[]{:S(2)}) copy-start(bf16[4,16,2,2,1024]{1,0,3,4,2:T(4,128)(2,1)} %copy.94) | copy-start | bytes 1572868
  385.2 6.9 %copy-start.9 = (bf16[8,256,1024]{1,0,2:T(8,128)(2,1)S(1)}, bf16[8,256,1024]{1,0,2:T(8,128)(2,1)}, u32[]{:S(2)}) copy-start(bf16[8,256,1024]{1,0,2:T(8,128)(2,1)} %copy.130) | copy-start | bytes 12582916
  437.9 9.0 %copy-start.2 = (bf16[8,256,1024]{1,0,2:T(8,128)(2,1)S(1)}, bf16[8,256,1024]{1,0,2:T(8,128)(2,1)}, u32[]{:S(2)}) copy-start(bf16[8,256,1024]{1,0,2:T(8,128)(2,1)} %copy.129) | copy-start | bytes 12582916
  499.7 10.0 %copy-start.3 = (bf16[8,256,1024]{1,0,2:T(8,128)(2,1)S(1)}, bf16[8,256,1024]{1,0,2:T(8,128)(2,1)}, u32[]{:S(2)}) copy-start(bf16[8,256,1024]{1,0,2:T(8,128)(2,1)} %copy.129) | copy-start | bytes 12582916
  499.7 9.9 %copy-start.6 = (bf16[4,16,2,2,1024]{1,0,3,4,2:T(4,128)(2,1)S(1)}, bf16[4,16,2,2,1024]{1,0,3,4,2:T(4,128)(2,1)}, u32[]{:S(2)}) copy-start(bf16[4,16,2,2,1024]{1,0,3,4,2:T(4,128)(2,1)} %copy.94) | copy-start | bytes 1572868
  509.6 6.9 %copy-start.10 = (bf16[8,256,1024]{1,0,2:T(8,128)(2,1)S(1)}, bf16[8,256,1024]{1,0,2:T(8,128)(2,1)}, u32[]{:S(2)}) copy-start(bf16[8,256,1024]{1,0,2:T(8,128)(2,1)} %copy.130) | copy-start | bytes 12582916
